TPU v7x, 32 devices: a whole 2x2x4 slice. The times are simulated.
32 devices in a mesh: section: 8 (over z, x), dp: 4 (over y, core).
Axes of the slice: x: 2, y: 2, z: 4, core: 2. Of those that a mesh axis runs over, the one named last changes fastest.
Arguments:
- section_inputs: bfloat16 [8, 768, 1152], P('section'), may hold values from -6 to 6
- mirror_held: bfloat16 [8, 768, 1152], P('section'), may hold values from -6 to 6
- section_cotangents: bfloat16 [8, 768, 1152], P('section'), may hold values from -6 to 6
- next_batch: bfloat16 [768, 1152], replicated, may hold values from -6 to 6
- loss_cotangent: bfloat16 [768, 1152], replicated, may hold values from -6 to 6
- join_weights: bfloat16 [8, 1152, 1152], P('section'), may hold values from -0.125 to 0.125
Outputs:
- section_outputs: bfloat16 [32, 2, 768, 1152], P(('dp', 'section')), parts along dimension 0
- section_gradients: bfloat16 [32, 2, 768, 1152], P(('dp', 'section')), parts along dimension 0
- mirror_arrivals: bfloat16 [32, 768, 1152], P(('dp', 'section')), parts along dimension 0
There are 4 independent parts, one for each index of `dp`. A program takes and returns all parts, laid end to end along the dimension named above; an argument that names none is the same for every part. Nothing has to cross between parts.
All inputs are finite; a program needn't handle non-finite values.
Results may differ from a plain program's by a relative error of at most 0.001.
Values may be sent and summed in bfloat16 or wider, within the bound.
A program may use at most 128 MiB of HBM per device.

v0:
```python
import jax
import jax.numpy as jnp
from jax import lax
from jax.sharding import PartitionSpec as P


def from_partner(value, axis, bit):
    mask = 2**bit
    pairs = [(source, source ^ mask) for source in range(lax.axis_size(axis))]
    return lax.ppermute(value, axis, pairs)


def shifted(shard, axis, by):
    size = lax.axis_size(axis)
    pairs = [(i, i + by) for i in range(size) if 0 <= i + by < size]
    return lax.ppermute(shard, axis, pairs)


def to_mirror(payload):
    return from_partner(payload, "section", 0)


def pass_middle(payload, first_out, first_grad):
    return from_partner((payload, first_out, first_grad), "section", 0)


def local(
    section_inputs, mirror_held, section_cotangents, next_batch, loss_cotangent, join_weights
):
    count = lax.axis_size("section")
    position = lax.axis_index("section")
    is_early = position % 2 == 0
    weights = join_weights[0]

    def forward(arriving, pending):
        product = jnp.dot(arriving, weights, preferred_element_type=jnp.float32)
        joined = (product + pending.astype(jnp.float32)).astype(jnp.bfloat16)
        leaving = jnp.where(is_early, arriving, joined)
        return (leaving, product.astype(jnp.bfloat16))

    def backward(cotangent, returned):
        operand = jnp.where(is_early, returned, cotangent)
        product = lax.dot_general(
            operand, weights, (((1,), (1,)), ((), ())), preferred_element_type=jnp.float32
        )
        return jnp.where(is_early, cotangent.astype(jnp.float32) + product, product).astype(
            jnp.bfloat16
        )

    held = mirror_held[0]
    first_cot = section_cotangents[0]
    first_out, projected_one = forward(section_inputs[0], held)
    first_grad = backward(first_cot, held)
    combined, across_out, across_grad = pass_middle(
        jnp.where(is_early, projected_one, first_cot), first_out, first_grad
    )
    from_below = shifted((first_out, first_grad), "section", 2)
    from_above = shifted((first_out, first_grad), "section", -2)
    late_in = jnp.where(position == count - 1, across_out, from_above[0])
    second_in = jnp.where(position == 0, next_batch, jnp.where(is_early, from_below[0], late_in))
    second_out, projected_two = forward(second_in, combined)
    early_cot = jnp.where(position == count - 2, across_grad, from_above[1])
    second_cot = jnp.where(
        position == 1, loss_cotangent, jnp.where(is_early, early_cot, from_below[1])
    )
    second_grad = backward(second_cot, combined)
    arrivals = to_mirror(jnp.where(is_early, projected_two, second_cot))
    section_outputs = jnp.stack([first_out, second_out], axis=0)[None]
    section_gradients = jnp.stack([first_grad, second_grad], axis=0)[None]
    return (section_outputs, section_gradients, arrivals[None])


def solution(mesh):
    in_specs = (
        P("section", None, None),
        P("section", None, None),
        P("section", None, None),
        P(),
        P(),
        P("section", None, None),
    )
    out_specs = (
        P(("dp", "section"), None, None, None),
        P(("dp", "section"), None, None, None),
        P(("dp", "section"), None, None),
    )
    return jax.shard_map(local, mesh=mesh, in_specs=in_specs, out_specs=out_specs, check_vma=False)
```

profile of v0, /device:TPU:0, one launch (start us, length us, event | category | flops | bytes accessed | tf_op | source)
XLA Modules:
  0.0 181.7 jit_solution(5910683727646320105)
XLA Ops:
  0.6 0.0 copy-start
  0.7 1.7 copy-done
  2.4 0.0 copy-start.1
  2.4 0.0 copy-start.2
  2.4 0.0 copy-start.3
  2.4 6.2 %fusion = bf16[768,1152]{1,0:T(8,128)(2,1)} fusion(bf16[1,1152,1152]{2,1,0:T(8,128)(2,1)S(1)} %copy-done, bf16[1,768,1152]{2,1,0:T(8,128)(2,1)} %param.8, bf16[1,768,1152]{2,1,0:T(8,128)(2,1)} %param.7, pred[]{:T(512)S(6)} %eq.17), kind=kOutput, calls=%fused_computation.2 | convolution fusion | flops 2042855424 | bytes 7962625 | tf_op jit(solution)/shard_map/dot_general | solution.py:43
  8.6 6.2 %collective-permute-start.6 = (bf16[768,1152]{1,0:T(8,128)(2,1)}, bf16[768,1152]{1,0:T(8,128)(2,1)}, u32[]{:S(2)}, u32[]{:S(2)}) collective-permute-start(bf16[768,1152]{1,0:T(8,128)(2,1)} %fusion), channel_id=1, source_target_pairs={{0,8},{4,12},{8,16},{12,20},{16,24},{20,28},{1,9},{5,13},{9,17},{1... | collective-permute-start | bytes 5308424 | tf_op jit(solution)/shard_map/ppermute | solution.py:16
  14.7 1.3 collective-permute-start.5
  16.0 1.6 collective-permute-start.4
  17.6 0.0 copy-done.1
  17.6 0.0 copy-done.2
  17.6 0.0 copy-done.3
  17.6 4.3 %bitcast_select_fusion = (bf16[768,1152]{1,0:T(8,128)(2,1)}, bf16[768,1152]{1,0:T(8,128)(2,1)}) fusion(bf16[1,768,1152]{2,1,0:T(8,128)(2,1)S(1)} %copy-done.1, pred[]{:T(512)S(6)} %eq.17, bf16[1,768,1152]{2,1,0:T(8,128)(2,1)S(1)} %copy-done.2, bf16[1,768,1152]{2,1,0:T(8,128)(2,1)S(1)} %copy-done.3, bf16[1,1152,1152]{2,1,0:T(8,128)(2,1)S(1)} %copy-done), kind=kOutput, calls=%fused_computation.22 | convolution fusion | flops 2043740160 | bytes 11501569 | tf_op jit(solution)/shard_map/dot_general | solution.py:36
  21.9 0.5 collective-permute-start.3
  22.4 1.3 collective-permute-start.2
  23.7 28.0 %collective-permute-done.6 = bf16[768,1152]{1,0:T(8,128)(2,1)} collective-permute-done((bf16[768,1152]{1,0:T(8,128)(2,1)}, bf16[768,1152]{1,0:T(8,128)(2,1)}, u32[]{:S(2)}, u32[]{:S(2)}) %collective-permute-start.6) | collective-permute-done | bytes 1769504 | tf_op jit(solution)/shard_map/ppermute | solution.py:16
  51.7 1.5 collective-permute-start.1
  53.2 5.3 %collective-permute-done.5 = bf16[768,1152]{1,0:T(8,128)(2,1)} collective-permute-done((bf16[768,1152]{1,0:T(8,128)(2,1)}, bf16[768,1152]{1,0:T(8,128)(2,1)}, u32[]{:S(2)}, u32[]{:S(2)}) %collective-permute-start.5) | collective-permute-done | bytes 1769504 | tf_op jit(solution)/shard_map/ppermute | solution.py:16
  58.5 3.5 %collective-permute-start = (bf16[768,1152]{1,0:T(8,128)(2,1)}, bf16[768,1152]{1,0:T(8,128)(2,1)}, u32[]{:S(2)}, u32[]{:S(2)}) collective-permute-start(bf16[768,1152]{1,0:T(8,128)(2,1)} %get-tuple-element.7), channel_id=1, source_target_pairs={{0,8},{4,12},{8,16},{12,20},{16,24},{20,28},{1,9},{5,13},{9,17},{1... | collective-permute-start | bytes 5308424 | tf_op jit(solution)/shard_map/ppermute | solution.py:16
  62.0 0.0 collective-permute-done.4
  62.0 33.9 %collective-permute-done.3 = bf16[768,1152]{1,0:T(8,128)(2,1)} collective-permute-done((bf16[768,1152]{1,0:T(8,128)(2,1)}, bf16[768,1152]{1,0:T(8,128)(2,1)}, u32[]{:S(2)}, u32[]{:S(2)}) %collective-permute-start.3) | collective-permute-done | bytes 1769504 | tf_op jit(solution)/shard_map/ppermute | solution.py:10
  95.9 0.0 collective-permute-done.2
  95.9 36.5 %collective-permute-done.1 = bf16[768,1152]{1,0:T(8,128)(2,1)} collective-permute-done((bf16[768,1152]{1,0:T(8,128)(2,1)}, bf16[768,1152]{1,0:T(8,128)(2,1)}, u32[]{:S(2)}, u32[]{:S(2)}) %collective-permute-start.1) | collective-permute-done | bytes 1769504 | tf_op jit(solution)/shard_map/ppermute | solution.py:10
  132.3 0.0 collective-permute-done
  132.3 8.9 %convert_select_fusion = (bf16[768,1152]{1,0:T(8,128)(2,1)S(1)}, bf16[768,1152]{1,0:T(8,128)(2,1)S(1)}, bf16[1,768,1152]{2,1,0:T(8,128)(2,1)S(1)}) fusion(pred[]{:T(512)S(6)} %eq.17, bf16[768,1152]{1,0:T(8,128)(2,1)} %param.10, bf16[768,1152]{1,0:T(8,128)(2,1)} %collective-permute-done.6, bf16[768,1152]{1,0:T(8,128)(2,1)} %collective-permute-done.4, ...), kind=kOutput, calls=%fused_computation.24 | convolution fusion | flops 2051702784 | bytes 23887876 | tf_op jit(solution)/shard_map/dot_general | solution.py:36
  141.3 1.6 collective-permute-start.7
  142.9 4.3 %fusion.15 = bf16[1,768,1152]{2,1,0:T(8,128)(2,1)S(1)} fusion(bf16[1,1152,1152]{2,1,0:T(8,128)(2,1)S(1)} %copy-done, bf16[768,1152]{1,0:T(8,128)(2,1)S(1)} %get-tuple-element.4, bf16[768,1152]{1,0:T(8,128)(2,1)} %collective-permute-done.3, pred[]{:T(512)S(6)} %eq.17), kind=kOutput, calls=%fused_computation.17 | convolution fusion | flops 2042855424 | bytes 7962625 | tf_op jit(solution)/shard_map/dot_general | solution.py:43
  147.2 4.8 %maximum_bitcast_fusion = (bf16[1,2,768,1152]{3,2,1,0:T(8,128)(2,1)}, bf16[1,2,768,1152]{3,2,1,0:T(8,128)(2,1)}) fusion(bf16[1,768,1152]{2,1,0:T(8,128)(2,1)S(1)} %get-tuple-element.5, bf16[1,768,1152]{2,1,0:T(8,128)(2,1)} %bitcast.3, bf16[1,768,1152]{2,1,0:T(8,128)(2,1)S(1)} %fusion.15, bf16[1,768,1152]{2,1,0:T(8,128)(2,1)} %bitcast.8), kind=kLoop, calls=%fused_computation.4 | loop fusion | flops 3538944 | bytes 14155776 | tf_op jit(solution)/shard_map/broadcast_in_dim | solution.py:68
  152.0 28.5 %collective-permute-done.7 = bf16[768,1152]{1,0:T(8,128)(2,1)S(1)} collective-permute-done((bf16[768,1152]{1,0:T(8,128)(2,1)S(1)}, bf16[768,1152]{1,0:T(8,128)(2,1)S(1)}, u32[]{:S(2)}, u32[]{:S(2)}) %collective-permute-start.7) | collective-permute-done | bytes 1769504 | tf_op jit(solution)/shard_map/ppermute | solution.py:10
  180.5 1.2 copy.10
Async XLA Ops:
  0.6 1.8 copy-start
  2.4 15.2 %copy-start.1 = (bf16[1,768,1152]{2,1,0:T(8,128)(2,1)S(1)}, bf16[1,768,1152]{2,1,0:T(8,128)(2,1)}, u32[]{:S(2)}) copy-start(bf16[1,768,1152]{2,1,0:T(8,128)(2,1)} %param.8) | copy-start | bytes 5308420
  2.4 15.2 %copy-start.2 = (bf16[1,768,1152]{2,1,0:T(8,128)(2,1)S(1)}, bf16[1,768,1152]{2,1,0:T(8,128)(2,1)}, u32[]{:S(2)}) copy-start(bf16[1,768,1152]{2,1,0:T(8,128)(2,1)} %param.7) | copy-start | bytes 5308420
  2.4 15.2 %copy-start.3 = (bf16[1,768,1152]{2,1,0:T(8,128)(2,1)S(1)}, bf16[1,768,1152]{2,1,0:T(8,128)(2,1)}, u32[]{:S(2)}) copy-start(bf16[1,768,1152]{2,1,0:T(8,128)(2,1)} %param.6) | copy-start | bytes 5308420
  8.6 43.1 %collective-permute-start.6 = (bf16[768,1152]{1,0:T(8,128)(2,1)}, bf16[768,1152]{1,0:T(8,128)(2,1)}, u32[]{:S(2)}, u32[]{:S(2)}) collective-permute-start(bf16[768,1152]{1,0:T(8,128)(2,1)} %fusion), channel_id=1, source_target_pairs={{0,8},{4,12},{8,16},{12,20},{16,24},{20,28},{1,9},{5,13},{9,17},{1... | collective-permute-start | bytes 5308424 | tf_op jit(solution)/shard_map/ppermute | solution.py:16
  14.7 43.7 %collective-permute-start.5 = (bf16[768,1152]{1,0:T(8,128)(2,1)}, bf16[768,1152]{1,0:T(8,128)(2,1)}, u32[]{:S(2)}, u32[]{:S(2)}) collective-permute-start(bf16[768,1152]{1,0:T(8,128)(2,1)} %fusion), channel_id=1, source_target_pairs={{8,0},{12,4},{16,8},{20,12},{24,16},{28,20},{9,1},{13,5},{17,9},{2... | collective-permute-start | bytes 5308424 | tf_op jit(solution)/shard_map/ppermute | solution.py:16
  16.0 45.9 %collective-permute-start.4 = (bf16[768,1152]{1,0:T(8,128)(2,1)}, bf16[768,1152]{1,0:T(8,128)(2,1)}, u32[]{:S(2)}, u32[]{:S(2)}) collective-permute-start(bf16[768,1152]{1,0:T(8,128)(2,1)} %fusion), channel_id=1, source_target_pairs={{0,4},{4,0},{8,12},{12,8},{16,20},{20,16},{24,28},{28,24},{1,5},{5... | collective-permute-start | bytes 5308424 | tf_op jit(solution)/shard_map/ppermute | solution.py:10
  21.9 74.0 %collective-permute-start.3 = (bf16[768,1152]{1,0:T(8,128)(2,1)}, bf16[768,1152]{1,0:T(8,128)(2,1)}, u32[]{:S(2)}, u32[]{:S(2)}) collective-permute-start(bf16[768,1152]{1,0:T(8,128)(2,1)} %get-tuple-element.6), channel_id=1, source_target_pairs={{0,4},{4,0},{8,12},{12,8},{16,20},{20,16},{24,28},{28,24},{1,5},{5... | collective-permute-start | bytes 5308424 | tf_op jit(solution)/shard_map/ppermute | solution.py:10
  22.4 73.5 %collective-permute-start.2 = (bf16[768,1152]{1,0:T(8,128)(2,1)}, bf16[768,1152]{1,0:T(8,128)(2,1)}, u32[]{:S(2)}, u32[]{:S(2)}) collective-permute-start(bf16[768,1152]{1,0:T(8,128)(2,1)} %get-tuple-element.7), channel_id=1, source_target_pairs={{8,0},{12,4},{16,8},{20,12},{24,16},{28,20},{9,1},{13,5},{17,9},{2... | collective-permute-start | bytes 5308424 | tf_op jit(solution)/shard_map/ppermute | solution.py:16
  51.7 80.6 %collective-permute-start.1 = (bf16[768,1152]{1,0:T(8,128)(2,1)}, bf16[768,1152]{1,0:T(8,128)(2,1)}, u32[]{:S(2)}, u32[]{:S(2)}) collective-permute-start(bf16[768,1152]{1,0:T(8,128)(2,1)} %get-tuple-element.7), channel_id=1, source_target_pairs={{0,4},{4,0},{8,12},{12,8},{16,20},{20,16},{24,28},{28,24},{1,5},{5... | collective-permute-start | bytes 5308424 | tf_op jit(solution)/shard_map/ppermute | solution.py:10
  58.5 73.8 %collective-permute-start = (bf16[768,1152]{1,0:T(8,128)(2,1)}, bf16[768,1152]{1,0:T(8,128)(2,1)}, u32[]{:S(2)}, u32[]{:S(2)}) collective-permute-start(bf16[768,1152]{1,0:T(8,128)(2,1)} %get-tuple-element.7), channel_id=1, source_target_pairs={{0,8},{4,12},{8,16},{12,20},{16,24},{20,28},{1,9},{5,13},{9,17},{1... | collective-permute-start | bytes 5308424 | tf_op jit(solution)/shard_map/ppermute | solution.py:16
  141.3 39.2 %collective-permute-start.7 = (bf16[768,1152]{1,0:T(8,128)(2,1)S(1)}, bf16[768,1152]{1,0:T(8,128)(2,1)S(1)}, u32[]{:S(2)}, u32[]{:S(2)}) collective-permute-start(bf16[768,1152]{1,0:T(8,128)(2,1)S(1)} %get-tuple-element.3), channel_id=1, source_target_pairs={{0,4},{4,0},{8,12},{12,8},{16,20},{20,16},{24,28},{28,24},{1,5},{5... | collective-permute-start | bytes 5308424 | tf_op jit(solution)/shard_map/ppermute | solution.py:10
where the time goes:
time: 182 us
  waiting for transfers between devices  132 us (73%)
  matrix products  23.7 us (13%)
  starting transfers between devices  17.4 us (10%)
  other arithmetic  4.82 us (3%)
  local copies, waits for them, and re-layouts  2.95 us (2%)
    ppermute x4, waiting for transfers between devices, from_partner(): return lax.ppermute(value, axis, pairs)  98.8 us
    ppermute x4, waiting for transfers between devices, shifted(): return lax.ppermute(shard, axis, pairs)  33.3 us
    dot_general x2, matrix products, forward(): product = jnp.dot(arriving, weights, preferred_element_type=jnp.float32)  13.2 us
    ppermute x4, starting transfers between devices, shifted(): return lax.ppermute(shard, axis, pairs)  12.2 us
    dot_general x2, matrix products, backward(): lax.dot_general(operand, weights, (((1,), (1,)), ((), ())), preferred_ele...  10.5 us
    ppermute x4, starting transfers between devices, from_partner(): return lax.ppermute(value, axis, pairs)  5.18 us
    broadcast_in_dim x1, other arithmetic, local(): section_outputs = jnp.stack([first_out, second_out], axis=0)[None]  4.82 us
  transfers between devices with their start and end apart: 8, of which 5 were waited for; matrix products, arithmetic and copies ran while one was open for 7% of the time, Pallas kernels for 0%

commit v1 on v0

v1 whole, which is shorter than its diff:
```python
import functools

import jax
import jax.numpy as jnp
from jax import lax
from jax.experimental import pallas as pl
from jax.experimental.pallas import tpu as pltpu
from jax.sharding import PartitionSpec as P

MESH = pl.DeviceIdType.MESH
CHUNKS = 2


def message_ids():
    ids = {}
    for kind in ("up", "down", "x1", "x2", "core_up", "fc", "fy", "ff", "ac", "ay", "af"):
        for i in range(CHUNKS):
            ids[kind, i] = len(ids)
    for kind in ("up_rest", "core_rest"):
        ids[kind] = len(ids)
    return ids


IDS = message_ids()


def kernel(
    count,
    a_hbm, h_hbm, g_hbm, nb_hbm, lc_hbm, w_hbm,
    out_hbm, grad_hbm, arr_hbm,
    a_v, h_v, g_v, w_v, uin, din, x1, fin, arr, y1, dx1, dx2, s1, s2,
    in_sem, out_sem, send_sem, recv_sem,
):
    rows, _ = a_v.shape
    half, quarter = rows // 2, rows // 4
    chunk = quarter // CHUNKS
    p = lax.axis_index("section")
    d = lax.axis_index("dp")
    mirror = p + 1 - 2 * (p % 2)
    core_peer = d + 1 - 2 * (d % 2)
    y_peer = d + 2 - 4 * ((d // 2) % 2)
    core, yy = d % 2, (d // 2) % 2
    is_even = p % 2 == 0
    is_odd = p % 2 == 1
    has_up = p + 2 < count
    is_top = p + 2 >= count
    has_down = p >= 2
    is_bottom = p < 2
    up = jnp.where(has_up, p + 2, p)
    down = jnp.where(has_down, p - 2, p)

    own = core * half + yy * quarter
    rest = core * half + (1 - yy) * quarter
    across = (1 - core) * half
    y_own = rest

    def rows_at(start, size):
        return pl.ds(pl.multiple_of(start, 16), size)

    def copy(src, dst, ks, kr, section, dp):
        return pltpu.make_async_remote_copy(
            src_ref=src, dst_ref=dst, send_sem=send_sem.at[ks], recv_sem=recv_sem.at[kr],
            device_id=(section, dp), device_id_type=MESH,
        )

    def landed(dst, key):
        k = IDS[key]
        copy(dst, dst, k, k, mirror, d).wait_recv()

    def sent(src, key):
        k = IDS[key]
        copy(src, src, k, k, mirror, d).wait_send()

    loads = [
        pltpu.make_async_copy(src, dst, in_sem.at[i])
        for i, (src, dst) in enumerate(
            ((w_hbm.at[0], w_v), (a_hbm.at[0], a_v), (g_hbm.at[0], g_v), (h_hbm.at[0], h_v))
        )
    ]
    w_load, a_load, g_load, h_load = loads
    for load in loads:
        load.start()
    nb_load = pltpu.make_async_copy(nb_hbm, uin, in_sem.at[4])
    lc_load = pltpu.make_async_copy(lc_hbm, uin, in_sem.at[4])

    @pl.when(p == 0)
    def _():
        nb_load.start()

    @pl.when(p == 1)
    def _():
        lc_load.start()

    barrier = pltpu.get_barrier_semaphore()
    for peer in ((mirror, d), (p, core_peer), (p, y_peer)):
        pl.semaphore_signal(barrier, inc=1, device_id=peer, device_id_type=MESH)

    @pl.when(has_up)
    def _():
        pl.semaphore_signal(barrier, inc=1, device_id=(up, d), device_id_type=MESH)

    @pl.when(has_down)
    def _():
        pl.semaphore_signal(barrier, inc=1, device_id=(down, d), device_id_type=MESH)

    pl.semaphore_wait(barrier, 3 + jnp.where(has_up, 1, 0) + jnp.where(has_down, 1, 0))

    def times_w(x):
        return jnp.dot(x, w_v[...], preferred_element_type=jnp.float32)

    def times_wt(x):
        return lax.dot_general(
            x, w_v[...], (((1,), (1,)), ((), ())), preferred_element_type=jnp.float32
        )

    def own_chunk(i):
        return rows_at(own + i * chunk, chunk)

    def send_up(src, i):
        @pl.when(has_up)
        def _():
            copy(src.at[own_chunk(i)], uin.at[own_chunk(i)], IDS["up", i], IDS["up", i], up, d).start()

        @pl.when(is_top)
        def _():
            copy(
                src.at[own_chunk(i)], din.at[pl.ds(i * chunk, chunk)],
                IDS["up", i], IDS["down", i], mirror, d,
            ).start()

    def send_up_rest(src):
        @pl.when(has_up)
        def _():
            r = rows_at(rest, quarter)
            copy(src.at[r], uin.at[r], IDS["up_rest"], IDS["up_rest"], up, d).start()

    def send_down(src, i):
        @pl.when(has_down)
        def _():
            copy(
                src.at[own_chunk(i)], din.at[pl.ds(i * chunk, chunk)],
                IDS["down", i], IDS["down", i], down, d,
            ).start()

    def send_x1(src, i):
        copy(src, x1.at[pl.ds(i * chunk, chunk)], IDS["x1", i], IDS["x1", i], mirror, d).start()

    def send_x2(src, i):
        copy(src, arr.at[own_chunk(i)], IDS["x2", i], IDS["x2", i], mirror, d).start()

    def back_even(r):
        prod = times_wt(h_v[r, :])
        dx1[r, :] = (g_v[r, :].astype(jnp.float32) + prod).astype(jnp.bfloat16)

    def back_odd(r):
        dx1[r, :] = times_wt(g_v[r, :]).astype(jnp.bfloat16)

    def forward_odd(r):
        y1[r, :] = (times_w(a_v[r, :]) + h_v[r, :].astype(jnp.float32)).astype(jnp.bfloat16)

    @pl.when(is_even)
    def _():
        for i in range(CHUNKS):
            send_up(a_hbm.at[0], i)
        w_load.wait()
        a_load.wait()

        @pl.loop(0, 1)
        def _(_i):
            s1[...] = times_w(a_v[rows_at(own, quarter), :]).astype(jnp.bfloat16)

        for i in range(CHUNKS):
            send_x1(s1.at[pl.ds(i * chunk, chunk)], i)
        g_load.wait()
        h_load.wait()
        back_even(rows_at(own, quarter))
        for i in range(CHUNKS):
            send_down(dx1, i)
        send_up_rest(a_hbm.at[0])

        pltpu.make_async_copy(a_v, out_hbm.at[0, 0], out_sem.at[0]).start()

        @pl.loop(1, 4)
        def _(k):
            back_even(rows_at(lax.rem(own + k * quarter, rows), quarter))

    @pl.when(is_odd)
    def _():
        for i in range(CHUNKS):
            send_x1(g_hbm.at[0].at[own_chunk(i)], i)
        w_load.wait()
        a_load.wait()
        g_load.wait()
        back_odd(rows_at(own, quarter))
        for i in range(CHUNKS):
            send_up(dx1, i)
        h_load.wait()
        forward_odd(rows_at(own, quarter))
        for i in range(CHUNKS):
            send_down(y1, i)

        @pl.loop(1, 4)
        def _(k):
            back_odd(rows_at(lax.rem(own + k * quarter, rows), quarter))

        send_up_rest(dx1)

        @pl.loop(1, 4)
        def _(k):
            forward_odd(rows_at(lax.rem(own + k * quarter, rows), quarter))

        pltpu.make_async_copy(y1, out_hbm.at[0, 0], out_sem.at[0]).start()

    pltpu.make_async_copy(dx1, grad_hbm.at[0, 0], out_sem.at[1]).start()

    @pl.when(is_bottom)
    def _():
        nb_load.wait()

    for i in range(CHUNKS):
        r, rc = own_chunk(i), pl.ds(i * chunk, chunk)

        @pl.when(has_down)
        def _():
            landed(uin.at[r], ("up", i))
            copy(
                uin.at[r], uin.at[r], IDS["core_up", i], IDS["core_up", i], p, core_peer
            ).start()

        @pl.when(is_even)
        def _():
            s2[rc, :] = times_w(uin[r, :]).astype(jnp.bfloat16)
            send_x2(s2.at[rc], i)

        @pl.when(is_odd)
        def _():
            send_x2(uin.at[r], i)

        landed(din.at[rc], ("down", i))
        landed(x1.at[rc], ("x1", i))

        @pl.when(is_even)
        def _():
            prod = times_wt(x1[rc, :])
            fin[r, :] = (din[rc, :].astype(jnp.float32) + prod).astype(jnp.bfloat16)

        @pl.when(is_odd)
        def _():
            prod = times_w(din[rc, :])
            fin[r, :] = (prod + x1[rc, :].astype(jnp.float32)).astype(jnp.bfloat16)

        copy(fin.at[r], fin.at[r], IDS["fy", i], IDS["fy", i], p, y_peer).start()
        copy(fin.at[r], fin.at[r], IDS["fc", i], IDS["fc", i], p, core_peer).start()

    def y_chunk(i):
        return rows_at(y_own + i * chunk, chunk)

    def pass_on(buf, got, key, i):
        r = y_chunk(i)
        landed(buf.at[r], (got, i))
        copy(buf.at[r], buf.at[r], IDS[key, i], IDS[key, i], p, core_peer).start()

    for i in range(CHUNKS):
        pass_on(fin, "fy", "ff", i)
        r = own_chunk(i)
        landed(arr.at[r], ("x2", i))
        copy(arr.at[r], arr.at[r], IDS["ay", i], IDS["ay", i], p, y_peer).start()
        copy(arr.at[r], arr.at[r], IDS["ac", i], IDS["ac", i], p, core_peer).start()

    @pl.when(has_down)
    def _():
        r = rows_at(rest, quarter)
        landed(uin.at[r], "up_rest")
        copy(uin.at[r], uin.at[r], IDS["core_rest"], IDS["core_rest"], p, core_peer).start()

    def joined_odd(r):
        dx2[r, :] = times_wt(uin[r, :]).astype(jnp.bfloat16)

    @pl.when(is_odd)
    def _():
        @pl.loop(0, 2)
        def _(k):
            joined_odd(rows_at(core * half + k * quarter, quarter))

    for i in range(CHUNKS):
        pass_on(arr, "ay", "af", i)

    @pl.when(has_down)
    def _():
        for i in range(CHUNKS):
            landed(uin.at[rows_at(across + yy * quarter + i * chunk, chunk)], ("core_up", i))
        landed(uin.at[rows_at(across + (1 - yy) * quarter, quarter)], "core_rest")

    @pl.when(is_odd)
    def _():
        @pl.loop(0, 2)
        def _(k):
            joined_odd(rows_at(across + k * quarter, quarter))

    for i in range(CHUNKS):
        landed(fin.at[rows_at(across + yy * quarter + i * chunk, chunk)], ("fc", i))
        landed(fin.at[rows_at(across + (1 - yy) * quarter + i * chunk, chunk)], ("ff", i))

    @pl.when(is_even)
    def _():
        pltpu.make_async_copy(uin, out_hbm.at[0, 1], out_sem.at[2]).start()
        pltpu.make_async_copy(fin, grad_hbm.at[0, 1], out_sem.at[3]).start()

    @pl.when(is_odd)
    def _():
        pltpu.make_async_copy(dx2, grad_hbm.at[0, 1], out_sem.at[2]).start()
        pltpu.make_async_copy(fin, out_hbm.at[0, 1], out_sem.at[3]).start()

    for i in range(CHUNKS):
        landed(arr.at[rows_at(across + yy * quarter + i * chunk, chunk)], ("ac", i))
        landed(arr.at[rows_at(across + (1 - yy) * quarter + i * chunk, chunk)], ("af", i))
    pltpu.make_async_copy(arr, arr_hbm.at[0], out_sem.at[4]).start()

    piece = x1.at[pl.ds(0, chunk)]
    for i in range(CHUNKS):
        for kind in ("up", "x1", "x2", "fc", "fy", "ff", "ac", "ay", "af"):
            sent(piece, (kind, i))

    @pl.when(has_up)
    def _():
        sent(x1, "up_rest")

    @pl.when(has_down)
    def _():
        for i in range(CHUNKS):
            sent(piece, ("down", i))
            sent(piece, ("core_up", i))
        sent(x1, "core_rest")

    for i in range(5):
        pltpu.make_async_copy(arr, arr_hbm.at[0], out_sem.at[i]).wait()


def local(count, a, h, g, nb, lc, w):
    _, rows, width = a.shape
    bf16 = jnp.bfloat16
    full = pltpu.VMEM((rows, width), bf16)
    quarter = pltpu.VMEM((rows // 4, width), bf16)
    anywhere = pl.BlockSpec(memory_space=pl.ANY)
    return pl.pallas_call(
        functools.partial(kernel, count),
        out_shape=(
            jax.ShapeDtypeStruct((1, 2, rows, width), bf16),
            jax.ShapeDtypeStruct((1, 2, rows, width), bf16),
            jax.ShapeDtypeStruct((1, rows, width), bf16),
        ),
        in_specs=[anywhere] * 6,
        out_specs=(anywhere,) * 3,
        scratch_shapes=[
            full, full, full, pltpu.VMEM((width, width), bf16),
            full, quarter, quarter, full, full, full, full, full, quarter, quarter,
            pltpu.SemaphoreType.DMA((5,)),
            pltpu.SemaphoreType.DMA((5,)),
            pltpu.SemaphoreType.DMA((len(IDS),)),
            pltpu.SemaphoreType.DMA((len(IDS),)),
        ],
        compiler_params=pltpu.CompilerParams(
            collective_id=0, has_side_effects=True, vmem_limit_bytes=48 * 1024 * 1024
        ),
        cost_estimate=pl.CostEstimate(
            flops=8 * rows * width * width,
            bytes_accessed=16 * rows * width + 2 * width * width,
            transcendentals=0,
        ),
    )(a, h, g, nb, lc, w)


def solution(mesh):
    in_specs = (
        P("section", None, None),
        P("section", None, None),
        P("section", None, None),
        P(),
        P(),
        P("section", None, None),
    )
    out_specs = (
        P(("dp", "section"), None, None, None),
        P(("dp", "section"), None, None, None),
        P(("dp", "section"), None, None),
    )
    return jax.shard_map(
        functools.partial(local, mesh.shape["section"]),
        mesh=mesh, in_specs=in_specs, out_specs=out_specs, check_vma=False,
    )
```

time: 182 us -> 54.1 us (0.30)
  the two profiles are of different devices: /device:TPU:0 before, /device:TPU:25 now
where the time goes in v1:
time: 54.1 us; the launch traced here: 53.1 us
  Pallas kernels  42.3 us (78%)
  local copies, waits for them, and re-layouts  10.2 us (19%)
  between operations  0.66 us (1%)
    pallas_call x1, Pallas kernels, local(): pl.pallas_call(functools.partial(kernel, count), out_shape=(jax.ShapeDtyp...  42.3 us
    unnamed x9, local copies, waits for them, and re-layouts  10.2 us

profile of v1, /device:TPU:25, one launch (start us, length us, event | category | flops | bytes accessed | tf_op | source)
XLA Modules:
  0.0 53.1 jit_solution(8246892997346726561)
XLA Ops:
  0.6 0.0 copy-start
  0.6 1.5 %copy-done = bf16[1,768,1152]{2,1,0:T(8,128)(2,1)S(1)} copy-done((bf16[1,768,1152]{2,1,0:T(8,128)(2,1)S(1)}, bf16[1,768,1152]{2,1,0:T(8,128)(2,1)}, u32[]{:S(2)}) %copy-start) | copy-done | bytes 1769496
  2.1 0.0 copy-start.1
  2.1 1.5 %copy-done.1 = bf16[1,768,1152]{2,1,0:T(8,128)(2,1)S(1)} copy-done((bf16[1,768,1152]{2,1,0:T(8,128)(2,1)S(1)}, bf16[1,768,1152]{2,1,0:T(8,128)(2,1)}, u32[]{:S(2)}) %copy-start.1) | copy-done | bytes 1769496
  3.6 42.3 %shard_map.85 = (bf16[1,2,768,1152]{3,2,1,0:T(8,128)(2,1)}, bf16[1,2,768,1152]{3,2,1,0:T(8,128)(2,1)}, bf16[1,768,1152]{2,1,0:T(8,128)(2,1)S(1)}) custom-call(bf16[1,768,1152]{2,1,0:T(8,128)(2,1)S(1)} %copy-done, bf16[1,768,1152]{2,1,0:T(8,128)(2,1)S(1)} %copy-done.1, bf16[1,768,1152]{2,1,0:T(8,128)(2,1)} %g_hbm.1, bf16[768,1152]{1,0:T(8,128)(2,1)} %nb_hbm.1, ...), custom_call_target="tpu_custom_call" | custom-call | flops 8153726976 | bytes 16809984 | tf_op jit(solution)/shard_map/pallas_call | solution.py:345
  45.9 0.0 copy-start.2
  45.9 4.2 %copy.12 = bf16[1,2,768,1152]{3,2,1,0:T(8,128)(2,1)} copy(bf16[1,2,768,1152]{3,2,1,0:T(8,128)(2,1)} %get-tuple-element.6) | data formatting | bytes 7077888
  50.1 0.0 copy-done.2
  50.1 1.8 %copy.13 = bf16[1,2,768,1152]{3,2,1,0:T(8,128)(2,1)} copy(bf16[1,2,768,1152]{3,2,1,0:T(8,128)(2,1)S(1)} %copy-done.2) | data formatting | bytes 7077888
  51.9 1.2 %copy.14 = bf16[1,768,1152]{2,1,0:T(8,128)(2,1)} copy(bf16[1,768,1152]{2,1,0:T(8,128)(2,1)S(1)} %get-tuple-element.8) | data formatting | bytes 3538944
Async XLA Ops:
  0.6 1.5 %copy-start = (bf16[1,768,1152]{2,1,0:T(8,128)(2,1)S(1)}, bf16[1,768,1152]{2,1,0:T(8,128)(2,1)}, u32[]{:S(2)}) copy-start(bf16[1,768,1152]{2,1,0:T(8,128)(2,1)} %a_hbm.1) | copy-start | bytes 5308420
  2.1 1.5 %copy-start.1 = (bf16[1,768,1152]{2,1,0:T(8,128)(2,1)S(1)}, bf16[1,768,1152]{2,1,0:T(8,128)(2,1)}, u32[]{:S(2)}) copy-start(bf16[1,768,1152]{2,1,0:T(8,128)(2,1)} %h_hbm.1) | copy-start | bytes 5308420
  45.9 4.2 %copy-start.2 = (bf16[1,2,768,1152]{3,2,1,0:T(8,128)(2,1)S(1)}, bf16[1,2,768,1152]{3,2,1,0:T(8,128)(2,1)}, u32[]{:S(2)}) copy-start(bf16[1,2,768,1152]{3,2,1,0:T(8,128)(2,1)} %get-tuple-element.7) | copy-start | bytes 10616836

commit v2 on v1

--- a/solution.py
+++ b/solution.py
@@ -8,7 +8,7 @@
 from jax.sharding import PartitionSpec as P
 
 MESH = pl.DeviceIdType.MESH
-CHUNKS = 2
+CHUNKS = 3
 
 
 def message_ids():
@@ -27,9 +27,9 @@
 def kernel(
     count,
     a_hbm, h_hbm, g_hbm, nb_hbm, lc_hbm, w_hbm,
-    out_hbm, grad_hbm, arr_hbm,
-    a_v, h_v, g_v, w_v, uin, din, x1, fin, arr, y1, dx1, dx2, s1, s2,
-    in_sem, out_sem, send_sem, recv_sem,
+    y1, dx1, uin, dx2, fin, arr,
+    a_v, h_v, g_v, w_v, din, x1, s1, s2,
+    in_sem, send_sem, recv_sem,
 ):
     rows, _ = a_v.shape
     half, quarter = rows // 2, rows // 4
@@ -82,6 +82,7 @@
         load.start()
     nb_load = pltpu.make_async_copy(nb_hbm, uin, in_sem.at[4])
     lc_load = pltpu.make_async_copy(lc_hbm, uin, in_sem.at[4])
+    y1_load = pltpu.make_async_copy(a_hbm.at[0], y1, in_sem.at[5])
 
     @pl.when(p == 0)
     def _():
@@ -158,99 +159,37 @@
     def forward_odd(r):
         y1[r, :] = (times_w(a_v[r, :]) + h_v[r, :].astype(jnp.float32)).astype(jnp.bfloat16)
 
+    def part(k):
+        return rows_at(lax.rem(own + k * quarter, rows), quarter)
+
     @pl.when(is_even)
     def _():
-        for i in range(CHUNKS):
-            send_up(a_hbm.at[0], i)
+        send_up(a_hbm.at[0], 0)
         w_load.wait()
         a_load.wait()
-
-        @pl.loop(0, 1)
-        def _(_i):
-            s1[...] = times_w(a_v[rows_at(own, quarter), :]).astype(jnp.bfloat16)
-
-        for i in range(CHUNKS):
-            send_x1(s1.at[pl.ds(i * chunk, chunk)], i)
+        s1[...] = times_w(a_v[rows_at(own, quarter), :]).astype(jnp.bfloat16)
+        send_x1(s1.at[pl.ds(0, chunk)], 0)
         g_load.wait()
         h_load.wait()
-        back_even(rows_at(own, quarter))
-        for i in range(CHUNKS):
-            send_down(dx1, i)
-        send_up_rest(a_hbm.at[0])
-
-        pltpu.make_async_copy(a_v, out_hbm.at[0, 0], out_sem.at[0]).start()
-
-        @pl.loop(1, 4)
-        def _(k):
-            back_even(rows_at(lax.rem(own + k * quarter, rows), quarter))
+        back_even(part(0))
+        send_down(dx1, 0)
+        y1_load.start()
 
     @pl.when(is_odd)
     def _():
-        for i in range(CHUNKS):
-            send_x1(g_hbm.at[0].at[own_chunk(i)], i)
+        send_x1(g_hbm.at[0].at[own_chunk(0)], 0)
         w_load.wait()
         a_load.wait()
         g_load.wait()
-        back_odd(rows_at(own, quarter))
-        for i in range(CHUNKS):
-            send_up(dx1, i)
+        back_odd(part(0))
+        send_up(dx1, 0)
         h_load.wait()
-        forward_odd(rows_at(own, quarter))
-        for i in range(CHUNKS):
-            send_down(y1, i)
-
-        @pl.loop(1, 4)
-        def _(k):
-            back_odd(rows_at(lax.rem(own + k * quarter, rows), quarter))
-
-        send_up_rest(dx1)
-
-        @pl.loop(1, 4)
-        def _(k):
-            forward_odd(rows_at(lax.rem(own + k * quarter, rows), quarter))
-
-        pltpu.make_async_copy(y1, out_hbm.at[0, 0], out_sem.at[0]).start()
-
-    pltpu.make_async_copy(dx1, grad_hbm.at[0, 0], out_sem.at[1]).start()
+        forward_odd(part(0))
+        send_down(y1, 0)
 
     @pl.when(is_bottom)
     def _():
         nb_load.wait()
-
-    for i in range(CHUNKS):
-        r, rc = own_chunk(i), pl.ds(i * chunk, chunk)
-
-        @pl.when(has_down)
-        def _():
-            landed(uin.at[r], ("up", i))
-            copy(
-                uin.at[r], uin.at[r], IDS["core_up", i], IDS["core_up", i], p, core_peer
-            ).start()
-
-        @pl.when(is_even)
-        def _():
-            s2[rc, :] = times_w(uin[r, :]).astype(jnp.bfloat16)
-            send_x2(s2.at[rc], i)
-
-        @pl.when(is_odd)
-        def _():
-            send_x2(uin.at[r], i)
-
-        landed(din.at[rc], ("down", i))
-        landed(x1.at[rc], ("x1", i))
-
-        @pl.when(is_even)
-        def _():
-            prod = times_wt(x1[rc, :])
-            fin[r, :] = (din[rc, :].astype(jnp.float32) + prod).astype(jnp.bfloat16)
-
-        @pl.when(is_odd)
-        def _():
-            prod = times_w(din[rc, :])
-            fin[r, :] = (prod + x1[rc, :].astype(jnp.float32)).astype(jnp.bfloat16)
-
-        copy(fin.at[r], fin.at[r], IDS["fy", i], IDS["fy", i], p, y_peer).start()
-        copy(fin.at[r], fin.at[r], IDS["fc", i], IDS["fc", i], p, core_peer).start()
 
     def y_chunk(i):
         return rows_at(y_own + i * chunk, chunk)
@@ -260,12 +199,98 @@
         landed(buf.at[r], (got, i))
         copy(buf.at[r], buf.at[r], IDS[key, i], IDS[key, i], p, core_peer).start()
 
-    for i in range(CHUNKS):
-        pass_on(fin, "fy", "ff", i)
-        r = own_chunk(i)
-        landed(arr.at[r], ("x2", i))
-        copy(arr.at[r], arr.at[r], IDS["ay", i], IDS["ay", i], p, y_peer).start()
-        copy(arr.at[r], arr.at[r], IDS["ac", i], IDS["ac", i], p, core_peer).start()
+    piece = x1.at[pl.ds(0, chunk)]
+    for i in range(CHUNKS + 1):
+        if i < CHUNKS:
+            r, rc = own_chunk(i), pl.ds(i * chunk, chunk)
+
+            @pl.when(is_even)
+            def _():
+                if i < 3:
+                    back_even(part(i + 1))
+
+            @pl.when(is_odd)
+            def _():
+                if i < 3:
+                    back_odd(part(i + 1))
+                    forward_odd(part(i + 1))
+
+            sent(piece, ("x1", i))
+            if i + 1 < CHUNKS:
+                @pl.when(is_even)
+                def _():
+                    send_x1(s1.at[pl.ds((i + 1) * chunk, chunk)], i + 1)
+
+                @pl.when(is_odd)
+                def _():
+                    send_x1(g_hbm.at[0].at[own_chunk(i + 1)], i + 1)
+
+            sent(piece, ("up", i))
+
+            @pl.when(is_even)
+            def _():
+                if i + 1 < CHUNKS:
+                    send_up(a_hbm.at[0], i + 1)
+                else:
+                    send_up_rest(a_hbm.at[0])
+
+            @pl.when(is_odd)
+            def _():
+                if i + 1 < CHUNKS:
+                    send_up(dx1, i + 1)
+                else:
+                    send_up_rest(dx1)
+
+            @pl.when(has_down)
+            def _():
+                sent(piece, ("down", i))
+                if i + 1 < CHUNKS:
+                    @pl.when(is_even)
+                    def _():
+                        send_down(dx1, i + 1)
+
+                    @pl.when(is_odd)
+                    def _():
+                        send_down(y1, i + 1)
+
+            @pl.when(has_down)
+            def _():
+                landed(uin.at[r], ("up", i))
+                k = IDS["core_up", i]
+                copy(uin.at[r], uin.at[r], k, k, p, core_peer).start()
+
+            @pl.when(is_even)
+            def _():
+                s2[rc, :] = times_w(uin[r, :]).astype(jnp.bfloat16)
+                send_x2(s2.at[rc], i)
+
+            @pl.when(is_odd)
+            def _():
+                send_x2(uin.at[r], i)
+
+            landed(din.at[rc], ("down", i))
+            landed(x1.at[rc], ("x1", i))
+
+            @pl.when(is_even)
+            def _():
+                prod = times_wt(x1[rc, :])
+                fin[r, :] = (din[rc, :].astype(jnp.float32) + prod).astype(jnp.bfloat16)
+
+            @pl.when(is_odd)
+            def _():
+                prod = times_w(din[rc, :])
+                fin[r, :] = (prod + x1[rc, :].astype(jnp.float32)).astype(jnp.bfloat16)
+
+            copy(fin.at[r], fin.at[r], IDS["fy", i], IDS["fy", i], p, y_peer).start()
+            copy(fin.at[r], fin.at[r], IDS["fc", i], IDS["fc", i], p, core_peer).start()
+        if i > 0:
+            r = own_chunk(i - 1)
+            landed(arr.at[r], ("x2", i - 1))
+            k = IDS["ay", i - 1]
+            copy(arr.at[r], arr.at[r], k, k, p, y_peer).start()
+            k = IDS["ac", i - 1]
+            copy(arr.at[r], arr.at[r], k, k, p, core_peer).start()
+            pass_on(fin, "fy", "ff", i - 1)
 
     @pl.when(has_down)
     def _():
@@ -282,7 +307,7 @@
         def _(k):
             joined_odd(rows_at(core * half + k * quarter, quarter))
 
-    for i in range(CHUNKS):
+    for i in range(CHUNKS - 1):
         pass_on(arr, "ay", "af", i)
 
     @pl.when(has_down)
@@ -297,28 +322,20 @@
         def _(k):
             joined_odd(rows_at(across + k * quarter, quarter))
 
+    pass_on(arr, "ay", "af", CHUNKS - 1)
     for i in range(CHUNKS):
         landed(fin.at[rows_at(across + yy * quarter + i * chunk, chunk)], ("fc", i))
         landed(fin.at[rows_at(across + (1 - yy) * quarter + i * chunk, chunk)], ("ff", i))
-
-    @pl.when(is_even)
-    def _():
-        pltpu.make_async_copy(uin, out_hbm.at[0, 1], out_sem.at[2]).start()
-        pltpu.make_async_copy(fin, grad_hbm.at[0, 1], out_sem.at[3]).start()
-
-    @pl.when(is_odd)
-    def _():
-        pltpu.make_async_copy(dx2, grad_hbm.at[0, 1], out_sem.at[2]).start()
-        pltpu.make_async_copy(fin, out_hbm.at[0, 1], out_sem.at[3]).start()
-
     for i in range(CHUNKS):
         landed(arr.at[rows_at(across + yy * quarter + i * chunk, chunk)], ("ac", i))
         landed(arr.at[rows_at(across + (1 - yy) * quarter + i * chunk, chunk)], ("af", i))
-    pltpu.make_async_copy(arr, arr_hbm.at[0], out_sem.at[4]).start()
-
-    piece = x1.at[pl.ds(0, chunk)]
+
+    @pl.when(is_even)
+    def _():
+        y1_load.wait()
+
     for i in range(CHUNKS):
-        for kind in ("up", "x1", "x2", "fc", "fy", "ff", "ac", "ay", "af"):
+        for kind in ("x2", "fc", "fy", "ff", "ac", "ay", "af"):
             sent(piece, (kind, i))
 
     @pl.when(has_up)
@@ -328,12 +345,28 @@
     @pl.when(has_down)
     def _():
         for i in range(CHUNKS):
-            sent(piece, ("down", i))
             sent(piece, ("core_up", i))
         sent(x1, "core_rest")
 
+
+def write_out(y1, dx1, uin, dx2, fin, arr, out_hbm, grad_hbm, arr_hbm, sem):
+    is_even = lax.axis_index("section") % 2 == 0
+    pltpu.make_async_copy(y1, out_hbm.at[0, 0], sem.at[0]).start()
+    pltpu.make_async_copy(dx1, grad_hbm.at[0, 0], sem.at[1]).start()
+    pltpu.make_async_copy(arr, arr_hbm.at[0], sem.at[2]).start()
+
+    @pl.when(is_even)
+    def _():
+        pltpu.make_async_copy(uin, out_hbm.at[0, 1], sem.at[3]).start()
+        pltpu.make_async_copy(fin, grad_hbm.at[0, 1], sem.at[4]).start()
+
+    @pl.when(jnp.logical_not(is_even))
+    def _():
+        pltpu.make_async_copy(dx2, grad_hbm.at[0, 1], sem.at[3]).start()
+        pltpu.make_async_copy(fin, out_hbm.at[0, 1], sem.at[4]).start()
+
     for i in range(5):
-        pltpu.make_async_copy(arr, arr_hbm.at[0], out_sem.at[i]).wait()
+        pltpu.make_async_copy(arr, arr_hbm.at[0], sem.at[i]).wait()
 
 
 def local(count, a, h, g, nb, lc, w):
@@ -341,33 +374,42 @@
     bf16 = jnp.bfloat16
     full = pltpu.VMEM((rows, width), bf16)
     quarter = pltpu.VMEM((rows // 4, width), bf16)
-    anywhere = pl.BlockSpec(memory_space=pl.ANY)
+    results = pl.pallas_call(
+        functools.partial(kernel, count),
+        out_shape=(full,) * 6,
+        in_specs=[pl.BlockSpec(memory_space=pltpu.HBM)] * 6,
+        out_specs=(pl.BlockSpec(memory_space=pltpu.VMEM),) * 6,
+        scratch_shapes=[
+            full, full, full, pltpu.VMEM((width, width), bf16),
+            quarter, quarter, quarter, quarter,
+            pltpu.SemaphoreType.DMA((6,)),
+            pltpu.SemaphoreType.DMA((len(IDS),)),
+            pltpu.SemaphoreType.DMA((len(IDS),)),
+        ],
+        compiler_params=pltpu.CompilerParams(
+            collective_id=0, has_side_effects=True, vmem_limit_bytes=52 * 1024 * 1024
+        ),
+        cost_estimate=pl.CostEstimate(
+            flops=8 * rows * width * width,
+            bytes_accessed=6 * rows * width + 2 * width * width,
+            transcendentals=0,
+        ),
+    )(a, h, g, nb, lc, w)
     return pl.pallas_call(
-        functools.partial(kernel, count),
+        write_out,
         out_shape=(
             jax.ShapeDtypeStruct((1, 2, rows, width), bf16),
             jax.ShapeDtypeStruct((1, 2, rows, width), bf16),
             jax.ShapeDtypeStruct((1, rows, width), bf16),
         ),
-        in_specs=[anywhere] * 6,
-        out_specs=(anywhere,) * 3,
-        scratch_shapes=[
-            full, full, full, pltpu.VMEM((width, width), bf16),
-            full, quarter, quarter, full, full, full, full, full, quarter, quarter,
-            pltpu.SemaphoreType.DMA((5,)),
-            pltpu.SemaphoreType.DMA((5,)),
-            pltpu.SemaphoreType.DMA((len(IDS),)),
-            pltpu.SemaphoreType.DMA((len(IDS),)),
-        ],
-        compiler_params=pltpu.CompilerParams(
-            collective_id=0, has_side_effects=True, vmem_limit_bytes=48 * 1024 * 1024
+        in_specs=[pl.BlockSpec(memory_space=pl.ANY)] * 6,
+        out_specs=(pl.BlockSpec(memory_space=pltpu.HBM),) * 3,
+        scratch_shapes=[pltpu.SemaphoreType.DMA((5,))],
+        compiler_params=pltpu.CompilerParams(vmem_limit_bytes=1024 * 1024),
+        cost_estimate=pl.CostEstimate(
+            flops=0, bytes_accessed=10 * rows * width, transcendentals=0
         ),
-        cost_estimate=pl.CostEstimate(
-            flops=8 * rows * width * width,
-            bytes_accessed=16 * rows * width + 2 * width * width,
-            transcendentals=0,
-        ),
-    )(a, h, g, nb, lc, w)
+    )(*results)
 
 
 def solution(mesh):

time: 54.1 us -> 44.7 us (0.83); the launches traced: 53.1 us -> 44.6 us
  local copies, waits for them, and re-layouts: 10.2 us -> 0 us
  Pallas kernels: 42.3 us -> 43.9 us
    unnamed x9 -> x0, local copies, waits for them, and re-layouts: 10.2 us -> none
    pallas_call x1 -> x2, Pallas kernels: 42.3 us -> 43.9 us  [the longest x1 40.4 us: local(): pl.pallas_call(functools.partial(kernel, count), out_shape=(full,) * 6, i...]
where the time goes in v2:
time: 44.7 us; the launch traced here: 44.6 us
  Pallas kernels  43.9 us (98%)
  between operations  0.64 us (1%)
    pallas_call x1, Pallas kernels, local(): pl.pallas_call(functools.partial(kernel, count), out_shape=(full,) * 6, i...  40.4 us
    pallas_call x1, Pallas kernels, local(): pl.pallas_call(write_out, out_shape=(jax.ShapeDtypeStruct((1, 2, rows, wi...  3.53 us

profile of v2, /device:TPU:25, one launch (start us, length us, event | category | flops | bytes accessed | tf_op | source)
XLA Modules:
  0.0 44.6 jit_solution(15560362074427978984)
XLA Ops:
  0.6 40.4 %shard_map.85 = (bf16[768,1152]{1,0:T(8,128)(2,1)S(1)}, bf16[768,1152]{1,0:T(8,128)(2,1)S(1)}, bf16[768,1152]{1,0:T(8,128)(2,1)S(1)}, bf16[768,1152]{1,0:T(8,128...) custom-call(bf16[1,768,1152]{2,1,0:T(8,128)(2,1)} %a_hbm.1, bf16[1,768,1152]{2,1,0:T(8,128)(2,1)} %h_hbm.1, ...), custom_call_target="tpu_custom_call" | custom-call | flops 8153726976 | bytes 7962624 | tf_op jit(solution)/shard_map/pallas_call | solution.py:377
  41.0 3.5 %shard_map.86 = (bf16[1,2,768,1152]{3,2,1,0:T(8,128)(2,1)}, bf16[1,2,768,1152]{3,2,1,0:T(8,128)(2,1)}, bf16[1,768,1152]{2,1,0:T(8,128)(2,1)}) custom-call(bf16[768,1152]{1,0:T(8,128)(2,1)S(1)} %get-tuple-element.9.y1, bf16[768,1152]{1,0:T(8,128)(2,1)S(1)} %get-tuple-element.10.dx1, bf16[768,1152]{1,0:T(8,128)(2,1)S(1)} %get-tuple-element.11.uin, ...), custom_call_target="tpu_custom_call" | custom-call | bytes 8847360 | tf_op jit(solution)/shard_map/pallas_call | solution.py:398

commit v3 on v2

--- a/solution.py
+++ b/solution.py
@@ -8,7 +8,8 @@
 from jax.sharding import PartitionSpec as P
 
 MESH = pl.DeviceIdType.MESH
-CHUNKS = 3
+CHUNKS = 4
+AHEAD = 2
 
 
 def message_ids():
@@ -159,33 +160,38 @@
     def forward_odd(r):
         y1[r, :] = (times_w(a_v[r, :]) + h_v[r, :].astype(jnp.float32)).astype(jnp.bfloat16)
 
-    def part(k):
-        return rows_at(lax.rem(own + k * quarter, rows), quarter)
+    parts = [rows_at(start, quarter) for start in (rest, across, across + quarter)]
 
     @pl.when(is_even)
     def _():
-        send_up(a_hbm.at[0], 0)
+        for i in range(AHEAD):
+            send_up(a_hbm.at[0], i)
         w_load.wait()
         a_load.wait()
         s1[...] = times_w(a_v[rows_at(own, quarter), :]).astype(jnp.bfloat16)
-        send_x1(s1.at[pl.ds(0, chunk)], 0)
+        for i in range(AHEAD):
+            send_x1(s1.at[pl.ds(i * chunk, chunk)], i)
         g_load.wait()
         h_load.wait()
-        back_even(part(0))
-        send_down(dx1, 0)
+        back_even(rows_at(own, quarter))
+        for i in range(AHEAD):
+            send_down(dx1, i)
         y1_load.start()
 
     @pl.when(is_odd)
     def _():
-        send_x1(g_hbm.at[0].at[own_chunk(0)], 0)
+        for i in range(AHEAD):
+            send_x1(g_hbm.at[0].at[own_chunk(i)], i)
         w_load.wait()
         a_load.wait()
         g_load.wait()
-        back_odd(part(0))
-        send_up(dx1, 0)
+        back_odd(rows_at(own, quarter))
+        for i in range(AHEAD):
+            send_up(dx1, i)
         h_load.wait()
-        forward_odd(part(0))
-        send_down(y1, 0)
+        forward_odd(rows_at(own, quarter))
+        for i in range(AHEAD):
+            send_down(y1, i)
 
     @pl.when(is_bottom)
     def _():
@@ -199,6 +205,9 @@
         landed(buf.at[r], (got, i))
         copy(buf.at[r], buf.at[r], IDS[key, i], IDS[key, i], p, core_peer).start()
 
+    def joined_odd(r):
+        dx2[r, :] = times_wt(uin[r, :]).astype(jnp.bfloat16)
+
     piece = x1.at[pl.ds(0, chunk)]
     for i in range(CHUNKS + 1):
         if i < CHUNKS:
@@ -207,51 +216,51 @@
             @pl.when(is_even)
             def _():
                 if i < 3:
-                    back_even(part(i + 1))
+                    back_even(parts[i])
 
             @pl.when(is_odd)
             def _():
                 if i < 3:
-                    back_odd(part(i + 1))
-                    forward_odd(part(i + 1))
+                    back_odd(parts[i])
+                    forward_odd(parts[i])
 
             sent(piece, ("x1", i))
-            if i + 1 < CHUNKS:
+            if i + AHEAD < CHUNKS:
                 @pl.when(is_even)
                 def _():
-                    send_x1(s1.at[pl.ds((i + 1) * chunk, chunk)], i + 1)
+                    send_x1(s1.at[pl.ds((i + AHEAD) * chunk, chunk)], i + AHEAD)
 
                 @pl.when(is_odd)
                 def _():
-                    send_x1(g_hbm.at[0].at[own_chunk(i + 1)], i + 1)
+                    send_x1(g_hbm.at[0].at[own_chunk(i + AHEAD)], i + AHEAD)
 
             sent(piece, ("up", i))
 
             @pl.when(is_even)
             def _():
-                if i + 1 < CHUNKS:
-                    send_up(a_hbm.at[0], i + 1)
-                else:
+                if i + AHEAD < CHUNKS:
+                    send_up(a_hbm.at[0], i + AHEAD)
+                elif i + AHEAD == CHUNKS:
                     send_up_rest(a_hbm.at[0])
 
             @pl.when(is_odd)
             def _():
-                if i + 1 < CHUNKS:
-                    send_up(dx1, i + 1)
-                else:
+                if i + AHEAD < CHUNKS:
+                    send_up(dx1, i + AHEAD)
+                elif i + AHEAD == CHUNKS:
                     send_up_rest(dx1)
 
             @pl.when(has_down)
             def _():
                 sent(piece, ("down", i))
-                if i + 1 < CHUNKS:
+                if i + AHEAD < CHUNKS:
                     @pl.when(is_even)
                     def _():
-                        send_down(dx1, i + 1)
+                        send_down(dx1, i + AHEAD)
 
                     @pl.when(is_odd)
                     def _():
-                        send_down(y1, i + 1)
+                        send_down(y1, i + AHEAD)
 
             @pl.when(has_down)
             def _():
@@ -291,36 +300,36 @@
             k = IDS["ac", i - 1]
             copy(arr.at[r], arr.at[r], k, k, p, core_peer).start()
             pass_on(fin, "fy", "ff", i - 1)
+        if i == CHUNKS - 1:
+            @pl.when(is_odd)
+            def _():
+                joined_odd(rows_at(own, quarter))
+
+    for i in range(CHUNKS - 2):
+        pass_on(arr, "ay", "af", i)
 
     @pl.when(has_down)
     def _():
         r = rows_at(rest, quarter)
         landed(uin.at[r], "up_rest")
         copy(uin.at[r], uin.at[r], IDS["core_rest"], IDS["core_rest"], p, core_peer).start()
-
-    def joined_odd(r):
-        dx2[r, :] = times_wt(uin[r, :]).astype(jnp.bfloat16)
-
-    @pl.when(is_odd)
-    def _():
-        @pl.loop(0, 2)
-        def _(k):
-            joined_odd(rows_at(core * half + k * quarter, quarter))
-
-    for i in range(CHUNKS - 1):
-        pass_on(arr, "ay", "af", i)
-
-    @pl.when(has_down)
-    def _():
         for i in range(CHUNKS):
             landed(uin.at[rows_at(across + yy * quarter + i * chunk, chunk)], ("core_up", i))
+
+    @pl.when(is_odd)
+    def _():
+        joined_odd(rows_at(rest, quarter))
+        joined_odd(rows_at(across + yy * quarter, quarter))
+
+    pass_on(arr, "ay", "af", CHUNKS - 2)
+
+    @pl.when(has_down)
+    def _():
         landed(uin.at[rows_at(across + (1 - yy) * quarter, quarter)], "core_rest")
 
     @pl.when(is_odd)
     def _():
-        @pl.loop(0, 2)
-        def _(k):
-            joined_odd(rows_at(across + k * quarter, quarter))
+        joined_odd(rows_at(across + (1 - yy) * quarter, quarter))
 
     pass_on(arr, "ay", "af", CHUNKS - 1)
     for i in range(CHUNKS):

time: 44.7 us -> 45.4 us (1.016)
  Pallas kernels: 43.9 us -> 44.4 us
    pallas_call x1, Pallas kernels: 40.4 us -> 40.9 us  [local(): pl.pallas_call(functools.partial(kernel, count), out_shape=(full,) * 6, i...]
where the time goes in v3:
time: 45.4 us; the launch traced here: 45.2 us
  Pallas kernels  44.4 us (98%)
  between operations  0.8 us (2%)
    pallas_call x1, Pallas kernels, local(): pl.pallas_call(functools.partial(kernel, count), out_shape=(full,) * 6, i...  40.9 us
    pallas_call x1, Pallas kernels, local(): pl.pallas_call(write_out, out_shape=(jax.ShapeDtypeStruct((1, 2, rows, wi...  3.53 us

profile of v3, /device:TPU:25, one launch (start us, length us, event | category | flops | bytes accessed | tf_op | source)
XLA Modules:
  0.0 45.2 jit_solution(6622051118561626335)
XLA Ops:
  0.6 40.9 %shard_map.85 = (bf16[768,1152]{1,0:T(8,128)(2,1)S(1)}, bf16[768,1152]{1,0:T(8,128)(2,1)S(1)}, bf16[768,1152]{1,0:T(8,128)(2,1)S(1)}, bf16[768,1152]{1,0:T(8,128...) custom-call(bf16[1,768,1152]{2,1,0:T(8,128)(2,1)} %a_hbm.1, bf16[1,768,1152]{2,1,0:T(8,128)(2,1)} %h_hbm.1, ...), custom_call_target="tpu_custom_call" | custom-call | flops 8153726976 | bytes 7962624 | tf_op jit(solution)/shard_map/pallas_call | solution.py:386
  41.5 3.5 %shard_map.86 = (bf16[1,2,768,1152]{3,2,1,0:T(8,128)(2,1)}, bf16[1,2,768,1152]{3,2,1,0:T(8,128)(2,1)}, bf16[1,768,1152]{2,1,0:T(8,128)(2,1)}) custom-call(bf16[768,1152]{1,0:T(8,128)(2,1)S(1)} %get-tuple-element.9.y1, bf16[768,1152]{1,0:T(8,128)(2,1)S(1)} %get-tuple-element.10.dx1, bf16[768,1152]{1,0:T(8,128)(2,1)S(1)} %get-tuple-element.11.uin, ...), custom_call_target="tpu_custom_call" | custom-call | bytes 8847360 | tf_op jit(solution)/shard_map/pallas_call | solution.py:407
